TPU v7x, 256 devices: a whole 4x4x8 slice. The times are simulated.
256 devices in a mesh: vocab: 32 (over y, z_hi, x), width: 8 (over z_lo, core).
Axes of the slice: x: 4, y: 4, z: 8 (z_hi: 2, z_lo: 4; z = z_hi * 4 + z_lo), core: 2. Of those that a mesh axis runs over, the one named last changes fastest.
Arguments:
- grad_rows: bfloat16 [8192, 5376], P('vocab', 'width'), may hold values from -6 to 6
- eigen_cols: bfloat16 [5376, 5376], P(None, 'width'), may hold values from -0.078125 to 0.078125
- first_moment: float32 [8192, 5376], P('vocab', 'width'), may hold values from -4 to 4
- second_moment: float32 [8192, 5376], P('vocab', 'width'), may hold values from 0.01 to 1
- params: bfloat16 [8192, 5376], P('vocab', 'width'), may hold values from -4 to 4
- covariance: float32 [5376, 5376], P('vocab', 'width'), may hold values from -6 to 6
Outputs:
- params_new: bfloat16 [8192, 5376], P('vocab', 'width')
- first_new: float32 [8192, 5376], P('vocab', 'width')
- second_new: float32 [8192, 5376], P('vocab', 'width')
- covariance_new: float32 [5376, 5376], P('vocab', 'width')
All inputs are finite; a program needn't handle non-finite values.
Results may differ from a plain program's by a relative error of at most 0.014.
Values may be sent and summed in bfloat16 or wider, within the bound.
No kernel may reach another device: no remote copies, remote signals or barrier semaphores. Data moves between devices by JAX's collectives and lax.ppermute only.
A program may use at most 128 MiB of HBM per device.

v0:
```python
import math

import jax
import jax.numpy as jnp
import numpy as np
from jax import lax
from jax.experimental import pallas as pl
from jax.experimental.pallas import tpu as pltpu
from jax.sharding import Mesh, PartitionSpec as P

BIAS_ONE = 1.0 - 0.9**10
BIAS_TWO = 1.0 - 0.95**10
BF16 = jnp.bfloat16
F32 = jnp.float32
COST_A = 16_000_000_000
COST_M = 11_000_000_000
COST_G = 1
COST_B = 10_000_000_000
COST_R = 10_000_000_000
COST_T = 1
COST_F = 20_000_000_000
AXES = ("y", "zh", "x", "zl", "c")
SIZES = (4, 2, 4, 4, 2)
IDS = np.arange(math.prod(SIZES)).reshape(SIZES)
CROSS = [r.tolist() for r in IDS[..., 0].transpose(0, 1, 3, 2).reshape(-1, 4)] + [
    r.tolist() for r in IDS[..., 1].transpose(1, 2, 3, 0).reshape(-1, 4)
]
CROSS_BACK = [r.tolist() for r in IDS[..., 0].transpose(1, 2, 3, 0).reshape(-1, 4)] + [
    r.tolist() for r in IDS[..., 1].transpose(0, 1, 3, 2).reshape(-1, 4)
]


def flip(a, axis, n, k):
    return lax.ppermute(a, axis, [(i, i ^ k) for i in range(n)])


def swap(a, groups):
    return lax.all_to_all(a, AXES, 0, 0, axis_index_groups=groups, tiled=True)


def route(a, target):
    pairs = []
    for i in range(IDS.size):
        to = target(*(int(k) for k in np.unravel_index(i, SIZES)))
        if to is not None:
            pairs.append((i, int(IDS[to])))
    return lax.ppermute(a, AXES, pairs)


def index(*at):
    return jnp.stack(at).astype(jnp.int32)


def pick(a, i, axis=0):
    return lax.dynamic_index_in_dim(a, i, axis, keepdims=False)


def spec(space=pltpu.VMEM):
    return pl.BlockSpec(memory_space=space)


def call(kernel, name, flops, out_shape, n_in, scratch=(), limit=8):
    return pl.pallas_call(
        kernel,
        out_shape=out_shape,
        in_specs=[spec(pltpu.SMEM)] + [spec()] * n_in,
        out_specs=jax.tree.map(lambda _: spec(), out_shape),
        scratch_shapes=scratch,
        compiler_params=pltpu.CompilerParams(vmem_limit_bytes=limit * 2**20),
        cost_estimate=pl.CostEstimate(flops=flops, bytes_accessed=1, transcendentals=0),
        name=name,
    )


def turn_kernel(a_ref, out_ref):
    out_ref[...] = a_ref[...].T


def turn(a):
    n, m = a.shape
    block = 1792
    return pl.pallas_call(
        turn_kernel,
        out_shape=jax.ShapeDtypeStruct((m, n), a.dtype),
        grid=(m // block,),
        in_specs=[pl.BlockSpec((n, block), lambda i: (0, i))],
        out_specs=pl.BlockSpec((block, n), lambda i: (i, 0)),
        compiler_params=pltpu.CompilerParams(vmem_limit_bytes=46 * 2**20),
        cost_estimate=pl.CostEstimate(flops=COST_T, bytes_accessed=1, transcendentals=0),
        name="turn",
    )(a)


def products_kernel(at_ref, l0, l1, l2, l3, early_ref, o0, o1, o2, o3, held):
    me, to = at_ref[0], at_ref[1]
    strip = held.shape[1]
    left = jnp.concatenate([l0[...], l1[...], l2[...], l3[...]], axis=1)
    for w in range(2):
        right = jnp.concatenate([early_ref[(me - d + 4) % 4, w] for d in range(4)], axis=1)
        total = lax.dot_general(
            left, right, (((1,), (1,)), ((), ())), preferred_element_type=F32
        )
        for j in range(4):
            held[j] = total[j * strip : (j + 1) * strip]
        for d, out in enumerate((o0, o1, o2, o3)):
            out[w] = held[(to + d) % 4].astype(BF16)


def products(at, late, early):
    cols = late[0].shape[0]
    out = jax.ShapeDtypeStruct((2, cols // 4, cols), BF16)
    held = pltpu.VMEM((4, cols // 4, cols), F32)
    return call(products_kernel, "products", COST_M, (out,) * 4, 5, [held], limit=20)(at, *late, early)


def add_kernel(at_ref, back_ref, got_ref, own_ref, *outs):
    c, z = at_ref[0], at_ref[1]
    total = [None] * 4
    for k in range(4):
        to = z ^ k
        value = back_ref[to, c].astype(F32) + got_ref[to].astype(F32)
        if k == 0:
            own_ref[...] = value
        else:
            outs[k - 1][...] = value.astype(BF16)


def add(at, back, got):
    shape = got.shape[1:]
    out = (jax.ShapeDtypeStruct(shape, F32),) + (jax.ShapeDtypeStruct(shape, BF16),) * 3
    return call(add_kernel, "add", 1, out, 2)(at, back, got)


def fold_kernel(at_ref, a, b, c, d, same_ref, other_ref):
    first = at_ref[0] == 0
    even = sum(r[0].astype(F32) for r in (a, b, c, d))
    odd = sum(r[1].astype(F32) for r in (a, b, c, d))
    same_ref[...] = jnp.where(first, even, odd)
    other_ref[...] = jnp.where(first, odd, even).astype(BF16)


def fold(at, parts):
    shape = parts[0].shape[1:]
    out = (jax.ShapeDtypeStruct(shape, F32), jax.ShapeDtypeStruct(shape, BF16))
    return call(fold_kernel, "fold", COST_G, out, 4)(at, *parts)


def choose_kernel(at_ref, same_ref, near_ref, keep_ref, give_ref):
    stays = at_ref[0] == at_ref[1]
    same, near = same_ref[...], near_ref[...].astype(F32)
    keep_ref[...] = jnp.where(stays, same, near)
    give_ref[...] = jnp.where(stays, near, same).astype(BF16)


def choose(at, same, near):
    out = (jax.ShapeDtypeStruct(same.shape, F32), jax.ShapeDtypeStruct(same.shape, BF16))
    return call(choose_kernel, "choose", COST_G, out, 2)(at, same, near)


def relay_kernel(at_ref, a, b, out_ref):
    out_ref[...] = (a[...].astype(F32) + b[...].astype(F32)).astype(BF16)


def relay(at, a, b):
    return call(relay_kernel, "relay", COST_R, jax.ShapeDtypeStruct(a.shape, BF16), 2)(at, a, b)


def finish_kernel(at_ref, p_ref, own, a, b, c, out_ref):
    total = own[...] + a[...].astype(F32) + b[...].astype(F32) + c[...].astype(F32)
    out_ref[...] = (p_ref[...].astype(F32) - 0.25 * total).astype(BF16)


def finish(at, params, pieces):
    out = jax.ShapeDtypeStruct(params.shape, BF16)
    return call(finish_kernel, "finish", COST_F, out, 5)(at, params, *pieces)


def gather_kernel(at_ref, alike, partner, o1, o2, o3, out_ref):
    z, c = at_ref[0], at_ref[1]
    for k in range(4):
        out_ref[k, c] = alike[k]
    for k, piece in enumerate((partner, o1, o2, o3)):
        out_ref[z ^ k, 1 - c] = piece[...]


def gather(at, alike, other):
    out = jax.ShapeDtypeStruct((4, 2) + alike.shape[1:], BF16)
    return call(gather_kernel, "gather", COST_B, out, 5)(at, alike, *other)


def arrange_kernel(at_ref, g, r1, r2, middle, edge, alike_ref, last_ref):
    z = at_ref[0]
    last = jnp.where((z == 1) | (z == 2), middle[...], edge[...])
    last_ref[...] = last
    alike_ref[z] = g[...]
    alike_ref[z ^ 1] = r1[...]
    alike_ref[z ^ 2] = r2[...]
    alike_ref[z ^ 3] = last


def arrange(at, pieces):
    shape = pieces[0].shape
    out = (jax.ShapeDtypeStruct((4,) + shape, BF16), jax.ShapeDtypeStruct(shape, BF16))
    return call(arrange_kernel, "arrange", COST_A, out, 5)(at, *pieces)


def local(grad_rows, eigen_cols, first_moment, second_moment, params, covariance):
    x, y = lax.axis_index("x"), lax.axis_index("y")
    h, z, c = lax.axis_index("zh"), lax.axis_index("zl"), lax.axis_index("c")
    vocab_total = grad_rows.shape[0] * 32

    g = grad_rows.T
    cols, rows = g.shape
    strip = cols // 4

    with jax.named_scope("early"):
        partner = flip(g, "c", 2, 1)
        across = [flip(g, "zl", 4, k) for k in (1, 2)]
        pair = jnp.where(c == 0, jnp.stack([g, partner]), jnp.stack([partner, g]))
        early = swap(jnp.broadcast_to(pair[None], (4,) + pair.shape), CROSS)
        by_rows = turn(eigen_cols.T)
        across[0], g_after, by_rows = lax.optimization_barrier((across[0], g, by_rows))
        middle = lax.ppermute(g_after, "zl", [(1, 2), (2, 1)])
        edge = lax.ppermute(across[1], "zl", [(1, 0), (2, 3)])
        alike, last = arrange(index(z), [g, *across, middle, edge])
        alike, last, early, by_rows = lax.optimization_barrier((alike, last, early, by_rows))

    with jax.named_scope("late"):
        by_strip = alike.reshape(4, 4, strip, rows)
        late = []
        for d in range(4):
            part = jnp.where(c == 0, pick(by_strip, (x + d) % 4, 1), pick(by_strip, (y + d) % 4, 0))
            if d > 0:
                part = route(
                    part,
                    lambda y, h, x, z, c: (y, h, (x + d) % 4, z, c) if c == 0 else ((y + d) % 4, h, x, z, c),
                )
            late.append(part.reshape(cols, rows))

    with jax.named_scope("cores"):
        other = [partner] + [flip(piece, "c", 2, 1) for piece in (*across, last)]
        full = gather(index(z, c), alike, other)
        flat = full.reshape(8 * cols, rows)

    with jax.named_scope("rotated"):
        rotated = lax.dot_general(
            eigen_cols, flat, (((0,), (0,)), ((), ())), preferred_element_type=F32
        )
        first_new = 0.9 * first_moment.T + 0.1 * rotated
        second_new = 0.95 * second_moment.T + 0.05 * rotated * rotated
        direction = (
            first_new / BIAS_ONE / (jnp.sqrt(second_new / BIAS_TWO) + 1e-08)
        ).astype(BF16)
        back = lax.dot_general(
            by_rows, direction, (((1,), (0,)), ((), ())), preferred_element_type=F32
        ).astype(BF16).reshape(4, 2, cols, rows)
        send = pick(back, 1 - c, 1)
        own, *both = add(index(c, z), back, flip(send, "c", 2, 1))

    with jax.named_scope("gram"):
        parts = products(index(jnp.where(c == 0, x, y), jnp.where(c == 0, y, x)), late, early)
        parts, both = lax.optimization_barrier((list(parts), both))

    with jax.named_scope("back"):
        one, two, three = both
        passed = lax.ppermute(three, "zl", [(0, 1), (3, 2)])
        middle = lax.ppermute(three, "zl", [(1, 2), (2, 1)])
        two = relay(index(z), two, passed)
        one, passed, middle = lax.optimization_barrier((one, passed, middle))
        got = [own, flip(one, "zl", 4, 1), flip(two, "zl", 4, 2), middle]

    with jax.named_scope("gram"):
        for d in (1, 2, 3):
            parts[d] = route(
                parts[d],
                lambda y, h, x, z, c: ((y + d) % 4, h, x, z, c) if c == 0 else (y, h, (x + d) % 4, z, c),
            )
        same, to_other = fold(index(c), parts)

    with jax.named_scope("finish"):
        params_new = finish(index(c), params.T, got)
        keep, give = choose(index(c, h), same, flip(to_other, "c", 2, 1))
        gram = keep + flip(give, "zh", 2, 1).astype(F32)
        covariance_new = 0.95 * covariance + gram * (1.0 / math.sqrt(vocab_total))
    return (params_new.T, first_new.T, second_new.T, covariance_new)


def solution(mesh):
    fine = Mesh(mesh.devices.reshape(SIZES), AXES)
    spec = P(("y", "zh", "x"), ("zl", "c"))
    return jax.shard_map(
        local,
        mesh=fine,
        in_specs=(spec, P(None, ("zl", "c")), spec, spec, spec, spec),
        out_specs=(spec, spec, spec, spec),
        check_vma=False,
    )
```

profile of v0, /device:TPU:16, one launch (start us, length us, event | category | flops | bytes accessed | tf_op | source)
XLA Modules:
  0.0 99.7 jit_solution(13530139829421266721)
XLA Ops:
  0.7 2.0 %collective-permute-start = (bf16[672,256]{1,0:T(8,128)(2,1)}, bf16[672,256]{1,0:T(8,128)(2,1)S(1)}, u32[]{:S(2)}, u32[]{:S(2)}) collective-permute-start(bf16[672,256]{1,0:T(8,128)(2,1)} %bitcast.70), channel_id=1, source_target_pairs={{0,2},{2,0},{4,6},{6,4},{1,3},{3,1},{5,7},{7,5},{8,10},{10,8},{12,... | collective-permute-start | bytes 1032200 | tf_op jit(solution)/shard_map/early/ppermute | solution.py:34
  2.7 3.3 %collective-permute-start.1 = (bf16[672,256]{1,0:T(8,128)(2,1)}, bf16[672,256]{1,0:T(8,128)(2,1)S(1)}, u32[]{:S(2)}, u32[]{:S(2)}) collective-permute-start(bf16[672,256]{1,0:T(8,128)(2,1)} %bitcast.71), channel_id=1, source_target_pairs={{0,4},{2,6},{4,0},{6,2},{1,5},{3,7},{5,1},{7,3},{8,12},{10,14},{12... | collective-permute-start | bytes 1032200 | tf_op jit(solution)/shard_map/early/ppermute | solution.py:34
  6.0 1.2 %maximum_select_fusion = bf16[2,672,256]{2,1,0:T(8,128)(2,1)S(1)} fusion(bf16[1,672,256]{2,1,0:T(8,128)(2,1)S(1)} %bitcast.75, bf16[1,672,256]{2,1,0:T(8,128)(2,1)} %bitcast.72, pred[]{:T(512)S(6)} %eq.18), kind=kLoop, calls=%fused_computation.10 | loop fusion | flops 1032192 | bytes 1376257 | tf_op jit(solution)/shard_map/early/jit(_where)/select_n | solution.py:219
  7.2 1.8 %broadcast_in_dim.2 = bf16[4,2,672,256]{3,2,1,0:T(8,128)(2,1)} broadcast(bf16[2,672,256]{2,1,0:T(8,128)(2,1)S(1)} %maximum_select_fusion), dimensions={1,2,3} | broadcast | bytes 3440640 | tf_op jit(solution)/shard_map/early/broadcast_in_dim | solution.py:220
  9.0 4.6 %all-to-all-start = ((bf16[4,2,672,256]{3,2,1,0:T(8,128)(2,1)}), bf16[4,2,672,256]{3,2,1,0:T(8,128)(2,1)}, u32[]{:S(2)}, u32[]{:S(2)}) async-start(bf16[4,2,672,256]{3,2,1,0:T(8,128)(2,1)} %broadcast_in_dim.2), calls=%async_computation | async-start | bytes 5505024 | tf_op jit(solution)/shard_map/early/all_to_all | solution.py:38
  13.7 3.0 %copy-done = bf16[5376,672]{0,1:T(8,128)(2,1)S(1)} copy-done((bf16[5376,672]{0,1:T(8,128)(2,1)S(1)}, bf16[5376,672]{0,1:T(8,128)(2,1)}, u32[]{:S(2)}) %copy-start) | copy-done | bytes 7225368
  16.7 5.0 %turn.1 = bf16[5376,672]{1,0:T(8,128)(2,1)} custom-call(bf16[672,5376]{1,0:T(8,128)(2,1)S(1)} %bitcast.61), custom_call_target="tpu_custom_call" | custom-call | flops 1 | bytes 1 | tf_op jit(solution)/shard_map/early/turn/pallas_call | solution.py:82
  22.4 1.3 %collective-permute-start.3 = (bf16[672,256]{1,0:T(8,128)(2,1)S(1)}, bf16[672,256]{1,0:T(8,128)(2,1)S(1)}, u32[]{:S(2)}, u32[]{:S(2)}) collective-permute-start(bf16[672,256]{1,0:T(8,128)(2,1)S(1)} %collective-permute-done.1.r2), channel_id=1, source_target_pairs={{2,0},{4,6},{3,1},{5,7},{10,8},{12,14},{11,9},{13,15},{18,16},{20,... | collective-permute-start | bytes 1032200 | tf_op jit(solution)/shard_map/early/ppermute | solution.py:224
  24.5 9.6 %collective-permute-done.3.edge = bf16[672,256]{1,0:T(8,128)(2,1)S(1)} collective-permute-done((bf16[672,256]{1,0:T(8,128)(2,1)S(1)}, bf16[672,256]{1,0:T(8,128)(2,1)S(1)}, u32[]{:S(2)}, u32[]{:S(2)}) %collective-permute-start.3) | collective-permute-done | bytes 344096 | tf_op jit(solution)/shard_map/early/ppermute | solution.py:224
  34.3 0.7 copy-done.3
  35.2 1.6 %collective-permute-start.9 = (bf16[4,168,256]{2,1,0:T(8,128)(2,1)S(1)}, bf16[4,168,256]{2,1,0:T(8,128)(2,1)S(1)}, u32[]{:S(2)}, u32[]{:S(2)}) collective-permute-start(bf16[4,168,256]{2,1,0:T(8,128)(2,1)S(1)} %get-tuple-element.65), channel_id=1, source_target_pairs={{0,8},{1,65},{2,10},{3,67},{4,12},{5,69},{6,14},{7,71},{8,16},{9,7... | collective-permute-start | bytes 1032200 | tf_op jit(solution)/shard_map/late/ppermute | solution.py:47
  36.8 2.7 %collective-permute-start.10 = (bf16[4,168,256]{2,1,0:T(8,128)(2,1)S(1)}, bf16[4,168,256]{2,1,0:T(8,128)(2,1)S(1)}, u32[]{:S(2)}, u32[]{:S(2)}) collective-permute-start(bf16[4,168,256]{2,1,0:T(8,128)(2,1)S(1)} %get-tuple-element.66), channel_id=1, source_target_pairs={{0,16},{1,129},{2,18},{3,131},{4,20},{5,133},{6,22},{7,135},{8,24}... | collective-permute-start | bytes 1032200 | tf_op jit(solution)/shard_map/late/ppermute | solution.py:47
  39.6 1.5 %collective-permute-start.11 = (bf16[4,168,256]{2,1,0:T(8,128)(2,1)S(1)}, bf16[4,168,256]{2,1,0:T(8,128)(2,1)S(1)}, u32[]{:S(2)}, u32[]{:S(2)}) collective-permute-start(bf16[4,168,256]{2,1,0:T(8,128)(2,1)S(1)} %get-tuple-element.64), channel_id=1, source_target_pairs={{0,24},{1,193},{2,26},{3,195},{4,28},{5,197},{6,30},{7,199},{8,0},... | collective-permute-start | bytes 1032200 | tf_op jit(solution)/shard_map/late/ppermute | solution.py:47
  41.1 2.0 %gather.1 = bf16[4,2,672,256]{3,2,1,0:T(8,128)(2,1)S(1)} custom-call(s32[2]{0:T(128)S(1)} %pad_add_fusion.1.at_ref, bf16[4,672,256]{2,1,0:T(8,128)(2,1)S(1)} %get-tuple-element.40.alike, bf16[672,256]{1,0:T(8,128)(2,1)S(1)} %collective-permute-done.4.partner, bf16[672,256]{1,0:T(8,128)(2,1)} %collective-permute-done.5.o1, ...), custom_call_target="tpu_custom_call" | custom-call | flops 10000000000 | bytes 1 | tf_op jit(solution)/shard_map/cores/gather/pallas_call | solution.py:188
  43.3 3.2 %fusion.5 = (f32[256,672]{0,1:T(8,128)}, f32[256,672]{0,1:T(8,128)}, f32[256,672]{0,1:T(8,128)S(1)}) fusion(f32[256,672]{0,1:T(8,128)S(1)} %copy-done.5, f32[256,672]{0,1:T(8,128)S(1)} %copy-done.6, bf16[5376,672]{0,1:T(8,128)(2,1)S(1)} %bitcast.63, bf16[5376,256]{1,0:T(8,128)(2,1)S(1)} %bitcast.80), kind=kOutput, calls=%fused_computation.9 | convolution fusion | flops 1850892288 | bytes 13418496 | tf_op jit(solution)/shard_map/rotated/dot_general | solution.py:246
  46.5 2.6 %convolution_convert_fusion = bf16[5376,256]{1,0:T(8,128)(2,1)S(1)} fusion(bf16[5376,672]{1,0:T(8,128)(2,1)S(1)} %bitcast.82, f32[256,672]{0,1:T(8,128)S(1)} %get-tuple-element.69, f32[256,672]{0,1:T(8,128)S(1)} %copy-done.5, f32[256,672]{0,1:T(8,128)S(1)} %copy-done.6), kind=kOutput, calls=%fused_computation | convolution fusion | flops 1853128704 | bytes 12042240 | tf_op jit(solution)/shard_map/rotated/dot_general | solution.py:254
  49.7 4.4 %products.1 = (bf16[2,168,672]{2,1,0:T(8,128)(2,1)S(1)}, bf16[2,168,672]{2,1,0:T(8,128)(2,1)S(1)}, bf16[2,168,672]{2,1,0:T(8,128)(2,1)S(1)}, bf16[2,168,672]{2,1,0:T(8,128)(2,1)S(1)}) custom-call(s32[2]{0:T(128)S(1)} %pad_add_fusion.2.at_ref, bf16[672,256]{1,0:T(8,128)(2,1)S(1)} %bitcast_select_fusion.3.l0, bf16[672,256]{1,0:T(8,128)(2,1)S(1)} %bitcast.77, ...), custom_call_target="tpu_custom_call" | custom-call | flops 11000000512 | bytes 1 | tf_op jit(solution)/shard_map/gram/products/pallas_call | solution.py:113
  54.1 0.9 add.172
  54.9 1.5 %collective-permute-start.12 = (bf16[672,256]{1,0:T(8,128)(2,1)S(1)}, bf16[672,256]{1,0:T(8,128)(2,1)S(1)}, u32[]{:S(2)}, u32[]{:S(2)}) collective-permute-start(bf16[672,256]{1,0:T(8,128)(2,1)S(1)} %get-tuple-element.52), channel_id=1, source_target_pairs={{0,2},{6,4},{1,3},{7,5},{8,10},{14,12},{9,11},{15,13},{16,18},{22,... | collective-permute-start | bytes 1032200 | tf_op jit(solution)/shard_map/back/ppermute | solution.py:266
  57.1 1.3 %collective-permute-start.16 = (bf16[2,168,672]{2,1,0:T(8,128)(2,1)S(1)}, bf16[2,168,672]{2,1,0:T(8,128)(2,1)S(1)}, u32[]{:S(2)}, u32[]{:S(2)}) collective-permute-start(bf16[2,168,672]{2,1,0:T(8,128)(2,1)S(1)} %get-tuple-element.57), channel_id=1, source_target_pairs={{0,64},{1,9},{2,66},{3,11},{4,68},{5,13},{6,70},{7,15},{8,72},{9,1... | collective-permute-start | bytes 1354760 | tf_op jit(solution)/shard_map/gram/ppermute | solution.py:47
  58.4 0.8 collective-permute-start.17
  59.2 1.1 %collective-permute-start.18 = (bf16[2,168,672]{2,1,0:T(8,128)(2,1)S(1)}, bf16[2,168,672]{2,1,0:T(8,128)(2,1)S(1)}, u32[]{:S(2)}, u32[]{:S(2)}) collective-permute-start(bf16[2,168,672]{2,1,0:T(8,128)(2,1)S(1)} %get-tuple-element.59), channel_id=1, source_target_pairs={{0,192},{1,25},{2,194},{3,27},{4,196},{5,29},{6,198},{7,31},{8,200... | collective-permute-start | bytes 1354760 | tf_op jit(solution)/shard_map/gram/ppermute | solution.py:47
  60.3 4.2 %collective-permute-done.12.b = bf16[672,256]{1,0:T(8,128)(2,1)S(1)} collective-permute-done((bf16[672,256]{1,0:T(8,128)(2,1)S(1)}, bf16[672,256]{1,0:T(8,128)(2,1)S(1)}, u32[]{:S(2)}, u32[]{:S(2)}) %collective-permute-start.12) | collective-permute-done | bytes 344096 | tf_op jit(solution)/shard_map/back/ppermute | solution.py:266
  64.5 2.9 %collective-permute-start.15 = (bf16[672,256]{1,0:T(8,128)(2,1)S(1)}, bf16[672,256]{1,0:T(8,128)(2,1)S(1)}, u32[]{:S(2)}, u32[]{:S(2)}) collective-permute-start(bf16[672,256]{1,0:T(8,128)(2,1)S(1)} %relay.1), channel_id=1, source_target_pairs={{0,4},{2,6},{4,0},{6,2},{1,5},{3,7},{5,1},{7,3},{8,12},{10,14},{12... | collective-permute-start | bytes 1032200 | tf_op jit(solution)/shard_map/back/ppermute | solution.py:34
  68.1 3.7 %collective-permute-done.17.c = bf16[2,168,672]{2,1,0:T(8,128)(2,1)S(1)} collective-permute-done((bf16[2,168,672]{2,1,0:T(8,128)(2,1)S(1)}, bf16[2,168,672]{2,1,0:T(8,128)(2,1)S(1)}, u32[]{:S(2)}, u32[]{:S(2)}) %collective-permute-start.17) | collective-permute-done | bytes 451616 | tf_op jit(solution)/shard_map/gram/ppermute | solution.py:47
  71.8 2.1 %collective-permute-done.18.d = bf16[2,168,672]{2,1,0:T(8,128)(2,1)S(1)} collective-permute-done((bf16[2,168,672]{2,1,0:T(8,128)(2,1)S(1)}, bf16[2,168,672]{2,1,0:T(8,128)(2,1)S(1)}, u32[]{:S(2)}, u32[]{:S(2)}) %collective-permute-start.18) | collective-permute-done | bytes 451616 | tf_op jit(solution)/shard_map/gram/ppermute | solution.py:47
  74.4 1.4 %collective-permute-done.19.near_ref = bf16[168,672]{1,0:T(8,128)(2,1)S(1)} collective-permute-done((bf16[168,672]{1,0:T(8,128)(2,1)S(1)}, bf16[168,672]{1,0:T(8,128)(2,1)S(1)}, u32[]{:S(2)}, u32[]{:S(2)}) %collective-permute-start.19) | collective-permute-done | bytes 225824 | tf_op jit(solution)/shard_map/finish/ppermute | solution.py:34
  76.5 5.3 %collective-permute-start.20 = (bf16[168,672]{1,0:T(8,128)(2,1)S(1)}, bf16[168,672]{1,0:T(8,128)(2,1)S(1)}, u32[]{:S(2)}, u32[]{:S(2)}) collective-permute-start(bf16[168,672]{1,0:T(8,128)(2,1)S(1)} %get-tuple-element.63), channel_id=1, source_target_pairs={{0,32},{32,0},{1,33},{33,1},{2,34},{34,2},{3,35},{35,3},{4,36},{36... | collective-permute-start | bytes 677384 | tf_op jit(solution)/shard_map/finish/ppermute | solution.py:34
  81.9 1.0 collective-permute-done.15.b
  82.9 2.0 %finish.1 = bf16[672,256]{1,0:T(8,128)(2,1)} custom-call(s32[1]{0:T(128)} %bitcast.at_ref, bf16[672,256]{1,0:T(8,128)(2,1)S(1)} %bitcast.76, f32[672,256]{1,0:T(8,128)S(1)} %get-tuple-element.42.own, bf16[672,256]{1,0:T(8,128)(2,1)} %collective-permute-done.14.a, bf16[672,256]{1,0:T(8,128)(2,1)S(1)} %collective-permute-done.15.b, ...), custom_call_target="tpu_custom_call" | custom-call | flops 20000000000 | bytes 1 | tf_op jit(solution)/shard_map/finish/finish/pallas_call | solution.py:175
  84.9 14.0 %collective-permute-done.20 = bf16[168,672]{1,0:T(8,128)(2,1)S(1)} collective-permute-done((bf16[168,672]{1,0:T(8,128)(2,1)S(1)}, bf16[168,672]{1,0:T(8,128)(2,1)S(1)}, u32[]{:S(2)}, u32[]{:S(2)}) %collective-permute-start.20) | collective-permute-done | bytes 225824 | tf_op jit(solution)/shard_map/finish/ppermute | solution.py:34
  98.8 0.9 multiply_add_fusion.1
  (59 shorter events, 5.2 us)
Async XLA Ops:
  0.6 5.4 %collective-permute-start.4 = (bf16[672,256]{1,0:T(8,128)(2,1)}, bf16[672,256]{1,0:T(8,128)(2,1)S(1)}, u32[]{:S(2)}, u32[]{:S(2)}) collective-permute-start(bf16[672,256]{1,0:T(8,128)(2,1)} %bitcast.69), channel_id=1, source_target_pairs={{0,1},{1,0},{2,3},{3,2},{4,5},{5,4},{6,7},{7,6},{8,9},{9,8},{10,11... | collective-permute-start | bytes 1032200 | tf_op jit(solution)/shard_map/early/ppermute | solution.py:34
  0.7 21.0 %collective-permute-start = (bf16[672,256]{1,0:T(8,128)(2,1)}, bf16[672,256]{1,0:T(8,128)(2,1)S(1)}, u32[]{:S(2)}, u32[]{:S(2)}) collective-permute-start(bf16[672,256]{1,0:T(8,128)(2,1)} %bitcast.70), channel_id=1, source_target_pairs={{0,2},{2,0},{4,6},{6,4},{1,3},{3,1},{5,7},{7,5},{8,10},{10,8},{12,... | collective-permute-start | bytes 1032200 | tf_op jit(solution)/shard_map/early/ppermute | solution.py:34
  2.7 19.7 %collective-permute-start.1 = (bf16[672,256]{1,0:T(8,128)(2,1)}, bf16[672,256]{1,0:T(8,128)(2,1)S(1)}, u32[]{:S(2)}, u32[]{:S(2)}) collective-permute-start(bf16[672,256]{1,0:T(8,128)(2,1)} %bitcast.71), channel_id=1, source_target_pairs={{0,4},{2,6},{4,0},{6,2},{1,5},{3,7},{5,1},{7,3},{8,12},{10,14},{12... | collective-permute-start | bytes 1032200 | tf_op jit(solution)/shard_map/early/ppermute | solution.py:34
  9.0 26.0 %all-to-all-start = ((bf16[4,2,672,256]{3,2,1,0:T(8,128)(2,1)}), bf16[4,2,672,256]{3,2,1,0:T(8,128)(2,1)}, u32[]{:S(2)}, u32[]{:S(2)}) async-start(bf16[4,2,672,256]{3,2,1,0:T(8,128)(2,1)} %broadcast_in_dim.2), calls=%async_computation | async-start | bytes 5505024 | tf_op jit(solution)/shard_map/early/all_to_all | solution.py:38
  13.6 3.1 %copy-start = (bf16[5376,672]{0,1:T(8,128)(2,1)S(1)}, bf16[5376,672]{0,1:T(8,128)(2,1)}, u32[]{:S(2)}) copy-start(bf16[5376,672]{0,1:T(8,128)(2,1)} %param.7) | copy-start | bytes 21676036
  16.7 5.0 %copy-start.1 = (bf16[256,672]{0,1:T(8,128)(2,1)S(1)}, bf16[256,672]{0,1:T(8,128)(2,1)}, u32[]{:S(2)}) copy-start(bf16[256,672]{0,1:T(8,128)(2,1)} %param.6) | copy-start | bytes 1032196
  21.7 2.8 %collective-permute-start.2 = (bf16[672,256]{1,0:T(8,128)(2,1)S(1)}, bf16[672,256]{1,0:T(8,128)(2,1)S(1)}, u32[]{:S(2)}, u32[]{:S(2)}) collective-permute-start(bf16[672,256]{1,0:T(8,128)(2,1)S(1)} %bitcast.73), channel_id=1, source_target_pairs={{2,4},{4,2},{3,5},{5,3},{10,12},{12,10},{11,13},{13,11},{18,20},{2... | collective-permute-start | bytes 1032200 | tf_op jit(solution)/shard_map/early/ppermute | solution.py:223
  22.4 11.7 %collective-permute-start.3 = (bf16[672,256]{1,0:T(8,128)(2,1)S(1)}, bf16[672,256]{1,0:T(8,128)(2,1)S(1)}, u32[]{:S(2)}, u32[]{:S(2)}) collective-permute-start(bf16[672,256]{1,0:T(8,128)(2,1)S(1)} %collective-permute-done.1.r2), channel_id=1, source_target_pairs={{2,0},{4,6},{3,1},{5,7},{10,8},{12,14},{11,9},{13,15},{18,16},{20,... | collective-permute-start | bytes 1032200 | tf_op jit(solution)/shard_map/early/ppermute | solution.py:224
  24.0 15.6 %collective-permute-start.5 = (bf16[672,256]{1,0:T(8,128)(2,1)S(1)}, bf16[672,256]{1,0:T(8,128)(2,1)}, u32[]{:S(2)}, u32[]{:S(2)}) collective-permute-start(bf16[672,256]{1,0:T(8,128)(2,1)S(1)} %collective-permute-done.r1), channel_id=1, source_target_pairs={{0,1},{1,0},{2,3},{3,2},{4,5},{5,4},{6,7},{7,6},{8,9},{9,8},{10,11... | collective-permute-start | bytes 1032200 | tf_op jit(solution)/shard_map/cores/ppermute | solution.py:34
  24.0 17.1 %collective-permute-start.6 = (bf16[672,256]{1,0:T(8,128)(2,1)S(1)}, bf16[672,256]{1,0:T(8,128)(2,1)}, u32[]{:S(2)}, u32[]{:S(2)}) collective-permute-start(bf16[672,256]{1,0:T(8,128)(2,1)S(1)} %collective-permute-done.1.r2), channel_id=1, source_target_pairs={{0,1},{1,0},{2,3},{3,2},{4,5},{5,4},{6,7},{7,6},{8,9},{9,8},{10,11... | collective-permute-start | bytes 1032200 | tf_op jit(solution)/shard_map/cores/ppermute | solution.py:34
  35.0 6.1 %collective-permute-start.7 = (bf16[672,256]{1,0:T(8,128)(2,1)}, bf16[672,256]{1,0:T(8,128)(2,1)S(1)}, u32[]{:S(2)}, u32[]{:S(2)}) collective-permute-start(bf16[672,256]{1,0:T(8,128)(2,1)} %copy-done.3), channel_id=1, source_target_pairs={{0,1},{1,0},{2,3},{3,2},{4,5},{5,4},{6,7},{7,6},{8,9},{9,8},{10,11... | collective-permute-start | bytes 1032200 | tf_op jit(solution)/shard_map/cores/ppermute | solution.py:34
  35.1 11.4 %slice-start.2 = ((s8[8257536]{0:T(1024)(128)(4,1)}), s8[4194304]{0:T(1024)(128)(4,1)S(1)}, s32[]{:S(2)}) async-start(s8[8257536]{0:T(1024)(128)(4,1)} %bitcast.81), calls=%async_computation.3 | async-start | bytes 8388608
  35.2 14.4 %collective-permute-start.9 = (bf16[4,168,256]{2,1,0:T(8,128)(2,1)S(1)}, bf16[4,168,256]{2,1,0:T(8,128)(2,1)S(1)}, u32[]{:S(2)}, u32[]{:S(2)}) collective-permute-start(bf16[4,168,256]{2,1,0:T(8,128)(2,1)S(1)} %get-tuple-element.65), channel_id=1, source_target_pairs={{0,8},{1,65},{2,10},{3,67},{4,12},{5,69},{6,14},{7,71},{8,16},{9,7... | collective-permute-start | bytes 1032200 | tf_op jit(solution)/shard_map/late/ppermute | solution.py:47
  36.8 12.9 %collective-permute-start.10 = (bf16[4,168,256]{2,1,0:T(8,128)(2,1)S(1)}, bf16[4,168,256]{2,1,0:T(8,128)(2,1)S(1)}, u32[]{:S(2)}, u32[]{:S(2)}) collective-permute-start(bf16[4,168,256]{2,1,0:T(8,128)(2,1)S(1)} %get-tuple-element.66), channel_id=1, source_target_pairs={{0,16},{1,129},{2,18},{3,131},{4,20},{5,133},{6,22},{7,135},{8,24}... | collective-permute-start | bytes 1032200 | tf_op jit(solution)/shard_map/late/ppermute | solution.py:47
  39.6 3.6 %slice-start = ((s8[7225344]{0:T(1024)(128)(4,1)}), s8[4194304]{0:T(1024)(128)(4,1)S(1)}, s32[]{:S(2)}) async-start(s8[7225344]{0:T(1024)(128)(4,1)} %bitcast.62), calls=%async_computation.1 | async-start | bytes 8388608
  39.6 3.7 %slice-start.1 = ((s8[7225344]{0:T(1024)(128)(4,1)}), s8[3031040]{0:T(1024)(128)(4,1)S(1)}, s32[]{:S(2)}) async-start(s8[7225344]{0:T(1024)(128)(4,1)} %bitcast.62), calls=%async_computation.2 | async-start | bytes 6062080
  39.6 3.7 %copy-start.5 = (f32[256,672]{0,1:T(8,128)S(1)}, f32[256,672]{0,1:T(8,128)}, u32[]{:S(2)}) copy-start(f32[256,672]{0,1:T(8,128)} %param.9) | copy-start | bytes 2064388
  39.6 3.7 %copy-start.6 = (f32[256,672]{0,1:T(8,128)S(1)}, f32[256,672]{0,1:T(8,128)}, u32[]{:S(2)}) copy-start(f32[256,672]{0,1:T(8,128)} %param.8) | copy-start | bytes 2064388
  39.6 6.9 %slice-start.3 = ((s8[8257536]{0:T(1024)(128)(4,1)}), s8[4063232]{0:T(1024)(128)(4,1)S(1)}, s32[]{:S(2)}) async-start(s8[8257536]{0:T(1024)(128)(4,1)} %bitcast.81), calls=%async_computation.4 | async-start | bytes 8126464
  39.6 10.1 %collective-permute-start.11 = (bf16[4,168,256]{2,1,0:T(8,128)(2,1)S(1)}, bf16[4,168,256]{2,1,0:T(8,128)(2,1)S(1)}, u32[]{:S(2)}, u32[]{:S(2)}) collective-permute-start(bf16[4,168,256]{2,1,0:T(8,128)(2,1)S(1)} %get-tuple-element.64), channel_id=1, source_target_pairs={{0,24},{1,193},{2,26},{3,195},{4,28},{5,197},{6,30},{7,199},{8,0},... | collective-permute-start | bytes 1032200 | tf_op jit(solution)/shard_map/late/ppermute | solution.py:47
  49.2 4.8 %collective-permute-start.8 = (bf16[4,672,256]{2,1,0:T(8,128)(2,1)S(1)}, bf16[4,672,256]{2,1,0:T(8,128)(2,1)S(1)}, u32[]{:S(2)}, u32[]{:S(2)}) collective-permute-start(bf16[4,672,256]{2,1,0:T(8,128)(2,1)S(1)} %dynamic-slice_bitcast_fusion), channel_id=1, source_target_pairs={{0,1},{1,0},{2,3},{3,2},{4,5},{5,4},{6,7},{7,6},{8,9},{9,8},{10,11... | collective-permute-start | bytes 4128776 | tf_op jit(solution)/shard_map/rotated/ppermute | solution.py:34
  54.9 9.5 %collective-permute-start.12 = (bf16[672,256]{1,0:T(8,128)(2,1)S(1)}, bf16[672,256]{1,0:T(8,128)(2,1)S(1)}, u32[]{:S(2)}, u32[]{:S(2)}) collective-permute-start(bf16[672,256]{1,0:T(8,128)(2,1)S(1)} %get-tuple-element.52), channel_id=1, source_target_pairs={{0,2},{6,4},{1,3},{7,5},{8,10},{14,12},{9,11},{15,13},{16,18},{22,... | collective-permute-start | bytes 1032200 | tf_op jit(solution)/shard_map/back/ppermute | solution.py:266
  56.4 11.0 %collective-permute-start.13 = (bf16[672,256]{1,0:T(8,128)(2,1)S(1)}, bf16[672,256]{1,0:T(8,128)(2,1)S(1)}, u32[]{:S(2)}, u32[]{:S(2)}) collective-permute-start(bf16[672,256]{1,0:T(8,128)(2,1)S(1)} %get-tuple-element.52), channel_id=1, source_target_pairs={{2,4},{4,2},{3,5},{5,3},{10,12},{12,10},{11,13},{13,11},{18,20},{2... | collective-permute-start | bytes 1032200 | tf_op jit(solution)/shard_map/back/ppermute | solution.py:267
  57.1 11.0 %collective-permute-start.16 = (bf16[2,168,672]{2,1,0:T(8,128)(2,1)S(1)}, bf16[2,168,672]{2,1,0:T(8,128)(2,1)S(1)}, u32[]{:S(2)}, u32[]{:S(2)}) collective-permute-start(bf16[2,168,672]{2,1,0:T(8,128)(2,1)S(1)} %get-tuple-element.57), channel_id=1, source_target_pairs={{0,64},{1,9},{2,66},{3,11},{4,68},{5,13},{6,70},{7,15},{8,72},{9,1... | collective-permute-start | bytes 1354760 | tf_op jit(solution)/shard_map/gram/ppermute | solution.py:47
  58.4 13.4 %collective-permute-start.17 = (bf16[2,168,672]{2,1,0:T(8,128)(2,1)S(1)}, bf16[2,168,672]{2,1,0:T(8,128)(2,1)S(1)}, u32[]{:S(2)}, u32[]{:S(2)}) collective-permute-start(bf16[2,168,672]{2,1,0:T(8,128)(2,1)S(1)} %get-tuple-element.58), channel_id=1, source_target_pairs={{0,128},{1,17},{2,130},{3,19},{4,132},{5,21},{6,134},{7,23},{8,136... | collective-permute-start | bytes 1354760 | tf_op jit(solution)/shard_map/gram/ppermute | solution.py:47
  59.2 14.7 %collective-permute-start.18 = (bf16[2,168,672]{2,1,0:T(8,128)(2,1)S(1)}, bf16[2,168,672]{2,1,0:T(8,128)(2,1)S(1)}, u32[]{:S(2)}, u32[]{:S(2)}) collective-permute-start(bf16[2,168,672]{2,1,0:T(8,128)(2,1)S(1)} %get-tuple-element.59), channel_id=1, source_target_pairs={{0,192},{1,25},{2,194},{3,27},{4,196},{5,29},{6,198},{7,31},{8,200... | collective-permute-start | bytes 1354760 | tf_op jit(solution)/shard_map/gram/ppermute | solution.py:47
  64.5 18.3 %copy-start.2 = (bf16[256,672]{0,1:T(8,128)(2,1)S(1)}, bf16[256,672]{0,1:T(8,128)(2,1)}, u32[]{:S(2)}) copy-start(bf16[256,672]{0,1:T(8,128)(2,1)} %param.10) | copy-start | bytes 1032196
  64.5 18.3 %collective-permute-start.15 = (bf16[672,256]{1,0:T(8,128)(2,1)S(1)}, bf16[672,256]{1,0:T(8,128)(2,1)S(1)}, u32[]{:S(2)}, u32[]{:S(2)}) collective-permute-start(bf16[672,256]{1,0:T(8,128)(2,1)S(1)} %relay.1), channel_id=1, source_target_pairs={{0,4},{2,6},{4,0},{6,2},{1,5},{3,7},{5,1},{7,3},{8,12},{10,14},{12... | collective-permute-start | bytes 1032200 | tf_op jit(solution)/shard_map/back/ppermute | solution.py:34
  67.4 15.4 %collective-permute-start.14 = (bf16[672,256]{1,0:T(8,128)(2,1)S(1)}, bf16[672,256]{1,0:T(8,128)(2,1)}, u32[]{:S(2)}, u32[]{:S(2)}) collective-permute-start(bf16[672,256]{1,0:T(8,128)(2,1)S(1)} %get-tuple-element.53), channel_id=1, source_target_pairs={{0,2},{2,0},{4,6},{6,4},{1,3},{3,1},{5,7},{7,5},{8,10},{10,8},{12,... | collective-permute-start | bytes 1032200 | tf_op jit(solution)/shard_map/back/ppermute | solution.py:34
  74.2 1.6 %collective-permute-start.19 = (bf16[168,672]{1,0:T(8,128)(2,1)S(1)}, bf16[168,672]{1,0:T(8,128)(2,1)S(1)}, u32[]{:S(2)}, u32[]{:S(2)}) collective-permute-start(bf16[168,672]{1,0:T(8,128)(2,1)S(1)} %get-tuple-element.61), channel_id=1, source_target_pairs={{0,1},{1,0},{2,3},{3,2},{4,5},{5,4},{6,7},{7,6},{8,9},{9,8},{10,11... | collective-permute-start | bytes 677384 | tf_op jit(solution)/shard_map/finish/ppermute | solution.py:34
  76.5 22.3 %collective-permute-start.20 = (bf16[168,672]{1,0:T(8,128)(2,1)S(1)}, bf16[168,672]{1,0:T(8,128)(2,1)S(1)}, u32[]{:S(2)}, u32[]{:S(2)}) collective-permute-start(bf16[168,672]{1,0:T(8,128)(2,1)S(1)} %get-tuple-element.63), channel_id=1, source_target_pairs={{0,32},{32,0},{1,33},{33,1},{2,34},{34,2},{3,35},{35,3},{4,36},{36... | collective-permute-start | bytes 677384 | tf_op jit(solution)/shard_map/finish/ppermute | solution.py:34
  82.8 16.0 %copy-start.4 = (f32[168,672]{1,0:T(8,128)S(1)}, f32[168,672]{1,0:T(8,128)}, u32[]{:S(2)}) copy-start(f32[168,672]{1,0:T(8,128)} %param.11) | copy-start | bytes 1354756
  (1 other events, 0.7 us)
where the time goes:
time: 100 us; the launch traced here: 99.7 us
  waiting for transfers between devices  36 us (36%)
  starting transfers between devices  32.9 us (33%)
  Pallas kernels  15.4 us (15%)
  local copies, waits for them, and re-layouts  5.95 us (6%)
  matrix products  5.8 us (6%)
  other arithmetic  2.64 us (3%)
  between operations  1.04 us (1%)
    ppermute x11, waiting for transfers between devices, flip(): return lax.ppermute(a, axis, [(i, i ^ k) for i in range(n)])  16.4 us
    ppermute x11, starting transfers between devices, flip(): return lax.ppermute(a, axis, [(i, i ^ k) for i in range(n)])  15.2 us
    ppermute x1, waiting for transfers between devices, local(): edge = lax.ppermute(across[1], 'zl', [(1, 0), (2, 3)])  9.63 us
    ppermute x6, starting transfers between devices, route(): return lax.ppermute(a, AXES, pairs)  8.97 us
    ppermute x6, waiting for transfers between devices, route(): return lax.ppermute(a, AXES, pairs)  5.8 us
    pallas_call x1, Pallas kernels, turn(): pl.pallas_call(turn_kernel, out_shape=jax.ShapeDtypeStruct((m, n), a.dtyp...  5.01 us
    all_to_all x1, starting transfers between devices, swap(): return lax.all_to_all(a, AXES, 0, 0, axis_index_groups=groups, tiled=True)  4.63 us
    pallas_call x1, Pallas kernels, products(): call(products_kernel, 'products', COST_M, (out,) * 4, 5, [held], limit=20)  4.35 us
  transfers between devices with their start and end apart: 22, of which 7 were waited for; matrix products, arithmetic and copies ran while one was open for 10% of the time, Pallas kernels for 15%

commit v1 on v0

--- a/solution.py
+++ b/solution.py
@@ -59,7 +59,7 @@
     return pl.BlockSpec(memory_space=space)
 
 
-def call(kernel, name, flops, out_shape, n_in, scratch=(), limit=8):
+def call(kernel, name, flops, out_shape, n_in, scratch=(), limit=7):
     return pl.pallas_call(
         kernel,
         out_shape=out_shape,
@@ -110,7 +110,7 @@
     cols = late[0].shape[0]
     out = jax.ShapeDtypeStruct((2, cols // 4, cols), BF16)
     held = pltpu.VMEM((4, cols // 4, cols), F32)
-    return call(products_kernel, "products", COST_M, (out,) * 4, 5, [held], limit=20)(at, *late, early)
+    return call(products_kernel, "products", COST_M, (out,) * 4, 5, [held], limit=16)(at, *late, early)
 
 
 def add_kernel(at_ref, back_ref, got_ref, own_ref, *outs):

time: 100 us -> 100 us (level)
  no operation moved by 1% of the time
where the time goes in v1:
time: 100 us; the launch traced here: 99.7 us
  waiting for transfers between devices  36 us (36%)
  starting transfers between devices  32.9 us (33%)
  Pallas kernels  15.4 us (15%)
  local copies, waits for them, and re-layouts  5.95 us (6%)
  matrix products  5.8 us (6%)
  other arithmetic  2.64 us (3%)
  between operations  1.04 us (1%)
    ppermute x11, waiting for transfers between devices, flip(): return lax.ppermute(a, axis, [(i, i ^ k) for i in range(n)])  16.4 us
    ppermute x11, starting transfers between devices, flip(): return lax.ppermute(a, axis, [(i, i ^ k) for i in range(n)])  15.2 us
    ppermute x1, waiting for transfers between devices, local(): edge = lax.ppermute(across[1], 'zl', [(1, 0), (2, 3)])  9.63 us
    ppermute x6, starting transfers between devices, route(): return lax.ppermute(a, AXES, pairs)  8.97 us
    ppermute x6, waiting for transfers between devices, route(): return lax.ppermute(a, AXES, pairs)  5.8 us
    pallas_call x1, Pallas kernels, turn(): pl.pallas_call(turn_kernel, out_shape=jax.ShapeDtypeStruct((m, n), a.dtyp...  5.01 us
    all_to_all x1, starting transfers between devices, swap(): return lax.all_to_all(a, AXES, 0, 0, axis_index_groups=groups, tiled=True)  4.63 us
    pallas_call x1, Pallas kernels, products(): call(products_kernel, 'products', COST_M, (out,) * 4, 5, [held], limit=16)  4.35 us
  transfers between devices with their start and end apart: 22, of which 7 were waited for; matrix products, arithmetic and copies ran while one was open for 10% of the time, Pallas kernels for 15%

profile of v1, /device:TPU:16, one launch (start us, length us, event | category | flops | bytes accessed | tf_op | source)
XLA Modules:
  0.0 99.7 jit_solution(5732821828877283485)
XLA Ops:
  0.7 2.0 %collective-permute-start = (bf16[672,256]{1,0:T(8,128)(2,1)}, bf16[672,256]{1,0:T(8,128)(2,1)S(1)}, u32[]{:S(2)}, u32[]{:S(2)}) collective-permute-start(bf16[672,256]{1,0:T(8,128)(2,1)} %bitcast.70), channel_id=1, source_target_pairs={{0,2},{2,0},{4,6},{6,4},{1,3},{3,1},{5,7},{7,5},{8,10},{10,8},{12,... | collective-permute-start | bytes 1032200 | tf_op jit(solution)/shard_map/early/ppermute | solution.py:34
  2.7 3.3 %collective-permute-start.1 = (bf16[672,256]{1,0:T(8,128)(2,1)}, bf16[672,256]{1,0:T(8,128)(2,1)S(1)}, u32[]{:S(2)}, u32[]{:S(2)}) collective-permute-start(bf16[672,256]{1,0:T(8,128)(2,1)} %bitcast.71), channel_id=1, source_target_pairs={{0,4},{2,6},{4,0},{6,2},{1,5},{3,7},{5,1},{7,3},{8,12},{10,14},{12... | collective-permute-start | bytes 1032200 | tf_op jit(solution)/shard_map/early/ppermute | solution.py:34
  6.0 1.2 %maximum_select_fusion = bf16[2,672,256]{2,1,0:T(8,128)(2,1)S(1)} fusion(bf16[1,672,256]{2,1,0:T(8,128)(2,1)S(1)} %bitcast.75, bf16[1,672,256]{2,1,0:T(8,128)(2,1)} %bitcast.72, pred[]{:T(512)S(6)} %eq.18), kind=kLoop, calls=%fused_computation.10 | loop fusion | flops 1032192 | bytes 1376257 | tf_op jit(solution)/shard_map/early/jit(_where)/select_n | solution.py:219
  7.2 1.8 %broadcast_in_dim.2 = bf16[4,2,672,256]{3,2,1,0:T(8,128)(2,1)} broadcast(bf16[2,672,256]{2,1,0:T(8,128)(2,1)S(1)} %maximum_select_fusion), dimensions={1,2,3} | broadcast | bytes 3440640 | tf_op jit(solution)/shard_map/early/broadcast_in_dim | solution.py:220
  9.0 4.6 %all-to-all-start = ((bf16[4,2,672,256]{3,2,1,0:T(8,128)(2,1)}), bf16[4,2,672,256]{3,2,1,0:T(8,128)(2,1)}, u32[]{:S(2)}, u32[]{:S(2)}) async-start(bf16[4,2,672,256]{3,2,1,0:T(8,128)(2,1)} %broadcast_in_dim.2), calls=%async_computation | async-start | bytes 5505024 | tf_op jit(solution)/shard_map/early/all_to_all | solution.py:38
  13.7 3.0 %copy-done = bf16[5376,672]{0,1:T(8,128)(2,1)S(1)} copy-done((bf16[5376,672]{0,1:T(8,128)(2,1)S(1)}, bf16[5376,672]{0,1:T(8,128)(2,1)}, u32[]{:S(2)}) %copy-start) | copy-done | bytes 7225368
  16.7 5.0 %turn.1 = bf16[5376,672]{1,0:T(8,128)(2,1)} custom-call(bf16[672,5376]{1,0:T(8,128)(2,1)S(1)} %bitcast.61), custom_call_target="tpu_custom_call" | custom-call | flops 1 | bytes 1 | tf_op jit(solution)/shard_map/early/turn/pallas_call | solution.py:82
  22.4 1.3 %collective-permute-start.3 = (bf16[672,256]{1,0:T(8,128)(2,1)S(1)}, bf16[672,256]{1,0:T(8,128)(2,1)S(1)}, u32[]{:S(2)}, u32[]{:S(2)}) collective-permute-start(bf16[672,256]{1,0:T(8,128)(2,1)S(1)} %collective-permute-done.1.r2), channel_id=1, source_target_pairs={{2,0},{4,6},{3,1},{5,7},{10,8},{12,14},{11,9},{13,15},{18,16},{20,... | collective-permute-start | bytes 1032200 | tf_op jit(solution)/shard_map/early/ppermute | solution.py:224
  24.5 9.6 %collective-permute-done.3.edge = bf16[672,256]{1,0:T(8,128)(2,1)S(1)} collective-permute-done((bf16[672,256]{1,0:T(8,128)(2,1)S(1)}, bf16[672,256]{1,0:T(8,128)(2,1)S(1)}, u32[]{:S(2)}, u32[]{:S(2)}) %collective-permute-start.3) | collective-permute-done | bytes 344096 | tf_op jit(solution)/shard_map/early/ppermute | solution.py:224
  34.3 0.7 copy-done.3
  35.2 1.6 %collective-permute-start.9 = (bf16[4,168,256]{2,1,0:T(8,128)(2,1)S(1)}, bf16[4,168,256]{2,1,0:T(8,128)(2,1)S(1)}, u32[]{:S(2)}, u32[]{:S(2)}) collective-permute-start(bf16[4,168,256]{2,1,0:T(8,128)(2,1)S(1)} %get-tuple-element.65), channel_id=1, source_target_pairs={{0,8},{1,65},{2,10},{3,67},{4,12},{5,69},{6,14},{7,71},{8,16},{9,7... | collective-permute-start | bytes 1032200 | tf_op jit(solution)/shard_map/late/ppermute | solution.py:47
  36.8 2.7 %collective-permute-start.10 = (bf16[4,168,256]{2,1,0:T(8,128)(2,1)S(1)}, bf16[4,168,256]{2,1,0:T(8,128)(2,1)S(1)}, u32[]{:S(2)}, u32[]{:S(2)}) collective-permute-start(bf16[4,168,256]{2,1,0:T(8,128)(2,1)S(1)} %get-tuple-element.66), channel_id=1, source_target_pairs={{0,16},{1,129},{2,18},{3,131},{4,20},{5,133},{6,22},{7,135},{8,24}... | collective-permute-start | bytes 1032200 | tf_op jit(solution)/shard_map/late/ppermute | solution.py:47
  39.6 1.5 %collective-permute-start.11 = (bf16[4,168,256]{2,1,0:T(8,128)(2,1)S(1)}, bf16[4,168,256]{2,1,0:T(8,128)(2,1)S(1)}, u32[]{:S(2)}, u32[]{:S(2)}) collective-permute-start(bf16[4,168,256]{2,1,0:T(8,128)(2,1)S(1)} %get-tuple-element.64), channel_id=1, source_target_pairs={{0,24},{1,193},{2,26},{3,195},{4,28},{5,197},{6,30},{7,199},{8,0},... | collective-permute-start | bytes 1032200 | tf_op jit(solution)/shard_map/late/ppermute | solution.py:47
  41.1 2.0 %gather.1 = bf16[4,2,672,256]{3,2,1,0:T(8,128)(2,1)S(1)} custom-call(s32[2]{0:T(128)S(1)} %pad_add_fusion.1.at_ref, bf16[4,672,256]{2,1,0:T(8,128)(2,1)S(1)} %get-tuple-element.40.alike, bf16[672,256]{1,0:T(8,128)(2,1)S(1)} %collective-permute-done.4.partner, bf16[672,256]{1,0:T(8,128)(2,1)} %collective-permute-done.5.o1, ...), custom_call_target="tpu_custom_call" | custom-call | flops 10000000000 | bytes 1 | tf_op jit(solution)/shard_map/cores/gather/pallas_call | solution.py:188
  43.3 3.2 %fusion.5 = (f32[256,672]{0,1:T(8,128)}, f32[256,672]{0,1:T(8,128)}, f32[256,672]{0,1:T(8,128)S(1)}) fusion(f32[256,672]{0,1:T(8,128)S(1)} %copy-done.5, f32[256,672]{0,1:T(8,128)S(1)} %copy-done.6, bf16[5376,672]{0,1:T(8,128)(2,1)S(1)} %bitcast.63, bf16[5376,256]{1,0:T(8,128)(2,1)S(1)} %bitcast.80), kind=kOutput, calls=%fused_computation.9 | convolution fusion | flops 1850892288 | bytes 13418496 | tf_op jit(solution)/shard_map/rotated/dot_general | solution.py:246
  46.5 2.6 %convolution_convert_fusion = bf16[5376,256]{1,0:T(8,128)(2,1)S(1)} fusion(bf16[5376,672]{1,0:T(8,128)(2,1)S(1)} %bitcast.82, f32[256,672]{0,1:T(8,128)S(1)} %get-tuple-element.69, f32[256,672]{0,1:T(8,128)S(1)} %copy-done.5, f32[256,672]{0,1:T(8,128)S(1)} %copy-done.6), kind=kOutput, calls=%fused_computation | convolution fusion | flops 1853128704 | bytes 12042240 | tf_op jit(solution)/shard_map/rotated/dot_general | solution.py:254
  49.7 4.4 %products.1 = (bf16[2,168,672]{2,1,0:T(8,128)(2,1)S(1)}, bf16[2,168,672]{2,1,0:T(8,128)(2,1)S(1)}, bf16[2,168,672]{2,1,0:T(8,128)(2,1)S(1)}, bf16[2,168,672]{2,1,0:T(8,128)(2,1)S(1)}) custom-call(s32[2]{0:T(128)S(1)} %pad_add_fusion.2.at_ref, bf16[672,256]{1,0:T(8,128)(2,1)S(1)} %bitcast_select_fusion.3.l0, bf16[672,256]{1,0:T(8,128)(2,1)S(1)} %bitcast.77, ...), custom_call_target="tpu_custom_call" | custom-call | flops 11000000512 | bytes 1 | tf_op jit(solution)/shard_map/gram/products/pallas_call | solution.py:113
  54.1 0.9 add.172
  54.9 1.5 %collective-permute-start.12 = (bf16[672,256]{1,0:T(8,128)(2,1)S(1)}, bf16[672,256]{1,0:T(8,128)(2,1)S(1)}, u32[]{:S(2)}, u32[]{:S(2)}) collective-permute-start(bf16[672,256]{1,0:T(8,128)(2,1)S(1)} %get-tuple-element.52), channel_id=1, source_target_pairs={{0,2},{6,4},{1,3},{7,5},{8,10},{14,12},{9,11},{15,13},{16,18},{22,... | collective-permute-start | bytes 1032200 | tf_op jit(solution)/shard_map/back/ppermute | solution.py:266
  57.1 1.3 %collective-permute-start.16 = (bf16[2,168,672]{2,1,0:T(8,128)(2,1)S(1)}, bf16[2,168,672]{2,1,0:T(8,128)(2,1)S(1)}, u32[]{:S(2)}, u32[]{:S(2)}) collective-permute-start(bf16[2,168,672]{2,1,0:T(8,128)(2,1)S(1)} %get-tuple-element.57), channel_id=1, source_target_pairs={{0,64},{1,9},{2,66},{3,11},{4,68},{5,13},{6,70},{7,15},{8,72},{9,1... | collective-permute-start | bytes 1354760 | tf_op jit(solution)/shard_map/gram/ppermute | solution.py:47
  58.4 0.8 collective-permute-start.17
  59.2 1.1 %collective-permute-start.18 = (bf16[2,168,672]{2,1,0:T(8,128)(2,1)S(1)}, bf16[2,168,672]{2,1,0:T(8,128)(2,1)S(1)}, u32[]{:S(2)}, u32[]{:S(2)}) collective-permute-start(bf16[2,168,672]{2,1,0:T(8,128)(2,1)S(1)} %get-tuple-element.59), channel_id=1, source_target_pairs={{0,192},{1,25},{2,194},{3,27},{4,196},{5,29},{6,198},{7,31},{8,200... | collective-permute-start | bytes 1354760 | tf_op jit(solution)/shard_map/gram/ppermute | solution.py:47
  60.3 4.2 %collective-permute-done.12.b = bf16[672,256]{1,0:T(8,128)(2,1)S(1)} collective-permute-done((bf16[672,256]{1,0:T(8,128)(2,1)S(1)}, bf16[672,256]{1,0:T(8,128)(2,1)S(1)}, u32[]{:S(2)}, u32[]{:S(2)}) %collective-permute-start.12) | collective-permute-done | bytes 344096 | tf_op jit(solution)/shard_map/back/ppermute | solution.py:266
  64.5 2.9 %collective-permute-start.15 = (bf16[672,256]{1,0:T(8,128)(2,1)S(1)}, bf16[672,256]{1,0:T(8,128)(2,1)S(1)}, u32[]{:S(2)}, u32[]{:S(2)}) collective-permute-start(bf16[672,256]{1,0:T(8,128)(2,1)S(1)} %relay.1), channel_id=1, source_target_pairs={{0,4},{2,6},{4,0},{6,2},{1,5},{3,7},{5,1},{7,3},{8,12},{10,14},{12... | collective-permute-start | bytes 1032200 | tf_op jit(solution)/shard_map/back/ppermute | solution.py:34
  68.1 3.7 %collective-permute-done.17.c = bf16[2,168,672]{2,1,0:T(8,128)(2,1)S(1)} collective-permute-done((bf16[2,168,672]{2,1,0:T(8,128)(2,1)S(1)}, bf16[2,168,672]{2,1,0:T(8,128)(2,1)S(1)}, u32[]{:S(2)}, u32[]{:S(2)}) %collective-permute-start.17) | collective-permute-done | bytes 451616 | tf_op jit(solution)/shard_map/gram/ppermute | solution.py:47
  71.8 2.1 %collective-permute-done.18.d = bf16[2,168,672]{2,1,0:T(8,128)(2,1)S(1)} collective-permute-done((bf16[2,168,672]{2,1,0:T(8,128)(2,1)S(1)}, bf16[2,168,672]{2,1,0:T(8,128)(2,1)S(1)}, u32[]{:S(2)}, u32[]{:S(2)}) %collective-permute-start.18) | collective-permute-done | bytes 451616 | tf_op jit(solution)/shard_map/gram/ppermute | solution.py:47
  74.4 1.4 %collective-permute-done.19.near_ref = bf16[168,672]{1,0:T(8,128)(2,1)S(1)} collective-permute-done((bf16[168,672]{1,0:T(8,128)(2,1)S(1)}, bf16[168,672]{1,0:T(8,128)(2,1)S(1)}, u32[]{:S(2)}, u32[]{:S(2)}) %collective-permute-start.19) | collective-permute-done | bytes 225824 | tf_op jit(solution)/shard_map/finish/ppermute | solution.py:34
  76.5 5.3 %collective-permute-start.20 = (bf16[168,672]{1,0:T(8,128)(2,1)S(1)}, bf16[168,672]{1,0:T(8,128)(2,1)S(1)}, u32[]{:S(2)}, u32[]{:S(2)}) collective-permute-start(bf16[168,672]{1,0:T(8,128)(2,1)S(1)} %get-tuple-element.63), channel_id=1, source_target_pairs={{0,32},{32,0},{1,33},{33,1},{2,34},{34,2},{3,35},{35,3},{4,36},{36... | collective-permute-start | bytes 677384 | tf_op jit(solution)/shard_map/finish/ppermute | solution.py:34
  81.9 1.0 collective-permute-done.15.b
  82.9 2.0 %finish.1 = bf16[672,256]{1,0:T(8,128)(2,1)} custom-call(s32[1]{0:T(128)} %bitcast.at_ref, bf16[672,256]{1,0:T(8,128)(2,1)S(1)} %bitcast.76, f32[672,256]{1,0:T(8,128)S(1)} %get-tuple-element.42.own, bf16[672,256]{1,0:T(8,128)(2,1)} %collective-permute-done.14.a, bf16[672,256]{1,0:T(8,128)(2,1)S(1)} %collective-permute-done.15.b, ...), custom_call_target="tpu_custom_call" | custom-call | flops 20000000000 | bytes 1 | tf_op jit(solution)/shard_map/finish/finish/pallas_call | solution.py:175
  84.9 14.0 %collective-permute-done.20 = bf16[168,672]{1,0:T(8,128)(2,1)S(1)} collective-permute-done((bf16[168,672]{1,0:T(8,128)(2,1)S(1)}, bf16[168,672]{1,0:T(8,128)(2,1)S(1)}, u32[]{:S(2)}, u32[]{:S(2)}) %collective-permute-start.20) | collective-permute-done | bytes 225824 | tf_op jit(solution)/shard_map/finish/ppermute | solution.py:34
  98.8 0.9 multiply_add_fusion.1
  (59 shorter events, 5.2 us)
Async XLA Ops:
  0.6 5.4 %collective-permute-start.4 = (bf16[672,256]{1,0:T(8,128)(2,1)}, bf16[672,256]{1,0:T(8,128)(2,1)S(1)}, u32[]{:S(2)}, u32[]{:S(2)}) collective-permute-start(bf16[672,256]{1,0:T(8,128)(2,1)} %bitcast.69), channel_id=1, source_target_pairs={{0,1},{1,0},{2,3},{3,2},{4,5},{5,4},{6,7},{7,6},{8,9},{9,8},{10,11... | collective-permute-start | bytes 1032200 | tf_op jit(solution)/shard_map/early/ppermute | solution.py:34
  0.7 21.0 %collective-permute-start = (bf16[672,256]{1,0:T(8,128)(2,1)}, bf16[672,256]{1,0:T(8,128)(2,1)S(1)}, u32[]{:S(2)}, u32[]{:S(2)}) collective-permute-start(bf16[672,256]{1,0:T(8,128)(2,1)} %bitcast.70), channel_id=1, source_target_pairs={{0,2},{2,0},{4,6},{6,4},{1,3},{3,1},{5,7},{7,5},{8,10},{10,8},{12,... | collective-permute-start | bytes 1032200 | tf_op jit(solution)/shard_map/early/ppermute | solution.py:34
  2.7 19.7 %collective-permute-start.1 = (bf16[672,256]{1,0:T(8,128)(2,1)}, bf16[672,256]{1,0:T(8,128)(2,1)S(1)}, u32[]{:S(2)}, u32[]{:S(2)}) collective-permute-start(bf16[672,256]{1,0:T(8,128)(2,1)} %bitcast.71), channel_id=1, source_target_pairs={{0,4},{2,6},{4,0},{6,2},{1,5},{3,7},{5,1},{7,3},{8,12},{10,14},{12... | collective-permute-start | bytes 1032200 | tf_op jit(solution)/shard_map/early/ppermute | solution.py:34
  9.0 26.0 %all-to-all-start = ((bf16[4,2,672,256]{3,2,1,0:T(8,128)(2,1)}), bf16[4,2,672,256]{3,2,1,0:T(8,128)(2,1)}, u32[]{:S(2)}, u32[]{:S(2)}) async-start(bf16[4,2,672,256]{3,2,1,0:T(8,128)(2,1)} %broadcast_in_dim.2), calls=%async_computation | async-start | bytes 5505024 | tf_op jit(solution)/shard_map/early/all_to_all | solution.py:38
  13.6 3.1 %copy-start = (bf16[5376,672]{0,1:T(8,128)(2,1)S(1)}, bf16[5376,672]{0,1:T(8,128)(2,1)}, u32[]{:S(2)}) copy-start(bf16[5376,672]{0,1:T(8,128)(2,1)} %param.7) | copy-start | bytes 21676036
  16.7 5.0 %copy-start.1 = (bf16[256,672]{0,1:T(8,128)(2,1)S(1)}, bf16[256,672]{0,1:T(8,128)(2,1)}, u32[]{:S(2)}) copy-start(bf16[256,672]{0,1:T(8,128)(2,1)} %param.6) | copy-start | bytes 1032196
  21.7 2.8 %collective-permute-start.2 = (bf16[672,256]{1,0:T(8,128)(2,1)S(1)}, bf16[672,256]{1,0:T(8,128)(2,1)S(1)}, u32[]{:S(2)}, u32[]{:S(2)}) collective-permute-start(bf16[672,256]{1,0:T(8,128)(2,1)S(1)} %bitcast.73), channel_id=1, source_target_pairs={{2,4},{4,2},{3,5},{5,3},{10,12},{12,10},{11,13},{13,11},{18,20},{2... | collective-permute-start | bytes 1032200 | tf_op jit(solution)/shard_map/early/ppermute | solution.py:223
  22.4 11.7 %collective-permute-start.3 = (bf16[672,256]{1,0:T(8,128)(2,1)S(1)}, bf16[672,256]{1,0:T(8,128)(2,1)S(1)}, u32[]{:S(2)}, u32[]{:S(2)}) collective-permute-start(bf16[672,256]{1,0:T(8,128)(2,1)S(1)} %collective-permute-done.1.r2), channel_id=1, source_target_pairs={{2,0},{4,6},{3,1},{5,7},{10,8},{12,14},{11,9},{13,15},{18,16},{20,... | collective-permute-start | bytes 1032200 | tf_op jit(solution)/shard_map/early/ppermute | solution.py:224
  24.0 15.6 %collective-permute-start.5 = (bf16[672,256]{1,0:T(8,128)(2,1)S(1)}, bf16[672,256]{1,0:T(8,128)(2,1)}, u32[]{:S(2)}, u32[]{:S(2)}) collective-permute-start(bf16[672,256]{1,0:T(8,128)(2,1)S(1)} %collective-permute-done.r1), channel_id=1, source_target_pairs={{0,1},{1,0},{2,3},{3,2},{4,5},{5,4},{6,7},{7,6},{8,9},{9,8},{10,11... | collective-permute-start | bytes 1032200 | tf_op jit(solution)/shard_map/cores/ppermute | solution.py:34
  24.0 17.1 %collective-permute-start.6 = (bf16[672,256]{1,0:T(8,128)(2,1)S(1)}, bf16[672,256]{1,0:T(8,128)(2,1)}, u32[]{:S(2)}, u32[]{:S(2)}) collective-permute-start(bf16[672,256]{1,0:T(8,128)(2,1)S(1)} %collective-permute-done.1.r2), channel_id=1, source_target_pairs={{0,1},{1,0},{2,3},{3,2},{4,5},{5,4},{6,7},{7,6},{8,9},{9,8},{10,11... | collective-permute-start | bytes 1032200 | tf_op jit(solution)/shard_map/cores/ppermute | solution.py:34
  35.0 6.1 %collective-permute-start.7 = (bf16[672,256]{1,0:T(8,128)(2,1)}, bf16[672,256]{1,0:T(8,128)(2,1)S(1)}, u32[]{:S(2)}, u32[]{:S(2)}) collective-permute-start(bf16[672,256]{1,0:T(8,128)(2,1)} %copy-done.3), channel_id=1, source_target_pairs={{0,1},{1,0},{2,3},{3,2},{4,5},{5,4},{6,7},{7,6},{8,9},{9,8},{10,11... | collective-permute-start | bytes 1032200 | tf_op jit(solution)/shard_map/cores/ppermute | solution.py:34
  35.1 11.4 %slice-start.2 = ((s8[8257536]{0:T(1024)(128)(4,1)}), s8[4194304]{0:T(1024)(128)(4,1)S(1)}, s32[]{:S(2)}) async-start(s8[8257536]{0:T(1024)(128)(4,1)} %bitcast.81), calls=%async_computation.3 | async-start | bytes 8388608
  35.2 14.4 %collective-permute-start.9 = (bf16[4,168,256]{2,1,0:T(8,128)(2,1)S(1)}, bf16[4,168,256]{2,1,0:T(8,128)(2,1)S(1)}, u32[]{:S(2)}, u32[]{:S(2)}) collective-permute-start(bf16[4,168,256]{2,1,0:T(8,128)(2,1)S(1)} %get-tuple-element.65), channel_id=1, source_target_pairs={{0,8},{1,65},{2,10},{3,67},{4,12},{5,69},{6,14},{7,71},{8,16},{9,7... | collective-permute-start | bytes 1032200 | tf_op jit(solution)/shard_map/late/ppermute | solution.py:47
  36.8 12.9 %collective-permute-start.10 = (bf16[4,168,256]{2,1,0:T(8,128)(2,1)S(1)}, bf16[4,168,256]{2,1,0:T(8,128)(2,1)S(1)}, u32[]{:S(2)}, u32[]{:S(2)}) collective-permute-start(bf16[4,168,256]{2,1,0:T(8,128)(2,1)S(1)} %get-tuple-element.66), channel_id=1, source_target_pairs={{0,16},{1,129},{2,18},{3,131},{4,20},{5,133},{6,22},{7,135},{8,24}... | collective-permute-start | bytes 1032200 | tf_op jit(solution)/shard_map/late/ppermute | solution.py:47
  39.6 3.6 %slice-start = ((s8[7225344]{0:T(1024)(128)(4,1)}), s8[4194304]{0:T(1024)(128)(4,1)S(1)}, s32[]{:S(2)}) async-start(s8[7225344]{0:T(1024)(128)(4,1)} %bitcast.62), calls=%async_computation.1 | async-start | bytes 8388608
  39.6 3.7 %slice-start.1 = ((s8[7225344]{0:T(1024)(128)(4,1)}), s8[3031040]{0:T(1024)(128)(4,1)S(1)}, s32[]{:S(2)}) async-start(s8[7225344]{0:T(1024)(128)(4,1)} %bitcast.62), calls=%async_computation.2 | async-start | bytes 6062080
  39.6 3.7 %copy-start.5 = (f32[256,672]{0,1:T(8,128)S(1)}, f32[256,672]{0,1:T(8,128)}, u32[]{:S(2)}) copy-start(f32[256,672]{0,1:T(8,128)} %param.9) | copy-start | bytes 2064388
  39.6 3.7 %copy-start.6 = (f32[256,672]{0,1:T(8,128)S(1)}, f32[256,672]{0,1:T(8,128)}, u32[]{:S(2)}) copy-start(f32[256,672]{0,1:T(8,128)} %param.8) | copy-start | bytes 2064388
  39.6 6.9 %slice-start.3 = ((s8[8257536]{0:T(1024)(128)(4,1)}), s8[4063232]{0:T(1024)(128)(4,1)S(1)}, s32[]{:S(2)}) async-start(s8[8257536]{0:T(1024)(128)(4,1)} %bitcast.81), calls=%async_computation.4 | async-start | bytes 8126464
  39.6 10.1 %collective-permute-start.11 = (bf16[4,168,256]{2,1,0:T(8,128)(2,1)S(1)}, bf16[4,168,256]{2,1,0:T(8,128)(2,1)S(1)}, u32[]{:S(2)}, u32[]{:S(2)}) collective-permute-start(bf16[4,168,256]{2,1,0:T(8,128)(2,1)S(1)} %get-tuple-element.64), channel_id=1, source_target_pairs={{0,24},{1,193},{2,26},{3,195},{4,28},{5,197},{6,30},{7,199},{8,0},... | collective-permute-start | bytes 1032200 | tf_op jit(solution)/shard_map/late/ppermute | solution.py:47
  49.2 4.8 %collective-permute-start.8 = (bf16[4,672,256]{2,1,0:T(8,128)(2,1)S(1)}, bf16[4,672,256]{2,1,0:T(8,128)(2,1)S(1)}, u32[]{:S(2)}, u32[]{:S(2)}) collective-permute-start(bf16[4,672,256]{2,1,0:T(8,128)(2,1)S(1)} %dynamic-slice_bitcast_fusion), channel_id=1, source_target_pairs={{0,1},{1,0},{2,3},{3,2},{4,5},{5,4},{6,7},{7,6},{8,9},{9,8},{10,11... | collective-permute-start | bytes 4128776 | tf_op jit(solution)/shard_map/rotated/ppermute | solution.py:34
  54.9 9.5 %collective-permute-start.12 = (bf16[672,256]{1,0:T(8,128)(2,1)S(1)}, bf16[672,256]{1,0:T(8,128)(2,1)S(1)}, u32[]{:S(2)}, u32[]{:S(2)}) collective-permute-start(bf16[672,256]{1,0:T(8,128)(2,1)S(1)} %get-tuple-element.52), channel_id=1, source_target_pairs={{0,2},{6,4},{1,3},{7,5},{8,10},{14,12},{9,11},{15,13},{16,18},{22,... | collective-permute-start | bytes 1032200 | tf_op jit(solution)/shard_map/back/ppermute | solution.py:266
  56.4 11.0 %collective-permute-start.13 = (bf16[672,256]{1,0:T(8,128)(2,1)S(1)}, bf16[672,256]{1,0:T(8,128)(2,1)S(1)}, u32[]{:S(2)}, u32[]{:S(2)}) collective-permute-start(bf16[672,256]{1,0:T(8,128)(2,1)S(1)} %get-tuple-element.52), channel_id=1, source_target_pairs={{2,4},{4,2},{3,5},{5,3},{10,12},{12,10},{11,13},{13,11},{18,20},{2... | collective-permute-start | bytes 1032200 | tf_op jit(solution)/shard_map/back/ppermute | solution.py:267
  57.1 11.0 %collective-permute-start.16 = (bf16[2,168,672]{2,1,0:T(8,128)(2,1)S(1)}, bf16[2,168,672]{2,1,0:T(8,128)(2,1)S(1)}, u32[]{:S(2)}, u32[]{:S(2)}) collective-permute-start(bf16[2,168,672]{2,1,0:T(8,128)(2,1)S(1)} %get-tuple-element.57), channel_id=1, source_target_pairs={{0,64},{1,9},{2,66},{3,11},{4,68},{5,13},{6,70},{7,15},{8,72},{9,1... | collective-permute-start | bytes 1354760 | tf_op jit(solution)/shard_map/gram/ppermute | solution.py:47
  58.4 13.4 %collective-permute-start.17 = (bf16[2,168,672]{2,1,0:T(8,128)(2,1)S(1)}, bf16[2,168,672]{2,1,0:T(8,128)(2,1)S(1)}, u32[]{:S(2)}, u32[]{:S(2)}) collective-permute-start(bf16[2,168,672]{2,1,0:T(8,128)(2,1)S(1)} %get-tuple-element.58), channel_id=1, source_target_pairs={{0,128},{1,17},{2,130},{3,19},{4,132},{5,21},{6,134},{7,23},{8,136... | collective-permute-start | bytes 1354760 | tf_op jit(solution)/shard_map/gram/ppermute | solution.py:47
  59.2 14.7 %collective-permute-start.18 = (bf16[2,168,672]{2,1,0:T(8,128)(2,1)S(1)}, bf16[2,168,672]{2,1,0:T(8,128)(2,1)S(1)}, u32[]{:S(2)}, u32[]{:S(2)}) collective-permute-start(bf16[2,168,672]{2,1,0:T(8,128)(2,1)S(1)} %get-tuple-element.59), channel_id=1, source_target_pairs={{0,192},{1,25},{2,194},{3,27},{4,196},{5,29},{6,198},{7,31},{8,200... | collective-permute-start | bytes 1354760 | tf_op jit(solution)/shard_map/gram/ppermute | solution.py:47
  64.5 18.3 %copy-start.2 = (bf16[256,672]{0,1:T(8,128)(2,1)S(1)}, bf16[256,672]{0,1:T(8,128)(2,1)}, u32[]{:S(2)}) copy-start(bf16[256,672]{0,1:T(8,128)(2,1)} %param.10) | copy-start | bytes 1032196
  64.5 18.3 %collective-permute-start.15 = (bf16[672,256]{1,0:T(8,128)(2,1)S(1)}, bf16[672,256]{1,0:T(8,128)(2,1)S(1)}, u32[]{:S(2)}, u32[]{:S(2)}) collective-permute-start(bf16[672,256]{1,0:T(8,128)(2,1)S(1)} %relay.1), channel_id=1, source_target_pairs={{0,4},{2,6},{4,0},{6,2},{1,5},{3,7},{5,1},{7,3},{8,12},{10,14},{12... | collective-permute-start | bytes 1032200 | tf_op jit(solution)/shard_map/back/ppermute | solution.py:34
  67.4 15.4 %collective-permute-start.14 = (bf16[672,256]{1,0:T(8,128)(2,1)S(1)}, bf16[672,256]{1,0:T(8,128)(2,1)}, u32[]{:S(2)}, u32[]{:S(2)}) collective-permute-start(bf16[672,256]{1,0:T(8,128)(2,1)S(1)} %get-tuple-element.53), channel_id=1, source_target_pairs={{0,2},{2,0},{4,6},{6,4},{1,3},{3,1},{5,7},{7,5},{8,10},{10,8},{12,... | collective-permute-start | bytes 1032200 | tf_op jit(solution)/shard_map/back/ppermute | solution.py:34
  74.2 1.6 %collective-permute-start.19 = (bf16[168,672]{1,0:T(8,128)(2,1)S(1)}, bf16[168,672]{1,0:T(8,128)(2,1)S(1)}, u32[]{:S(2)}, u32[]{:S(2)}) collective-permute-start(bf16[168,672]{1,0:T(8,128)(2,1)S(1)} %get-tuple-element.61), channel_id=1, source_target_pairs={{0,1},{1,0},{2,3},{3,2},{4,5},{5,4},{6,7},{7,6},{8,9},{9,8},{10,11... | collective-permute-start | bytes 677384 | tf_op jit(solution)/shard_map/finish/ppermute | solution.py:34
  76.5 22.3 %collective-permute-start.20 = (bf16[168,672]{1,0:T(8,128)(2,1)S(1)}, bf16[168,672]{1,0:T(8,128)(2,1)S(1)}, u32[]{:S(2)}, u32[]{:S(2)}) collective-permute-start(bf16[168,672]{1,0:T(8,128)(2,1)S(1)} %get-tuple-element.63), channel_id=1, source_target_pairs={{0,32},{32,0},{1,33},{33,1},{2,34},{34,2},{3,35},{35,3},{4,36},{36... | collective-permute-start | bytes 677384 | tf_op jit(solution)/shard_map/finish/ppermute | solution.py:34
  82.8 16.0 %copy-start.4 = (f32[168,672]{1,0:T(8,128)S(1)}, f32[168,672]{1,0:T(8,128)}, u32[]{:S(2)}) copy-start(f32[168,672]{1,0:T(8,128)} %param.11) | copy-start | bytes 1354756
  (1 other events, 0.7 us)
